TPU v7x, 32 devices: a whole 2x2x4 slice. The times are simulated.
32 devices in a mesh: term: 4 (over z), doc: 8 (over y, x, core).
Axes of the slice: x: 2, y: 2, z: 4, core: 2. Of those that a mesh axis runs over, the one named last changes fastest.
Arguments:
- postings: bfloat16 [4096, 30720], P('doc', 'term'), may hold values from 0 to 3
- query_terms: int32 [128, 32], replicated, may hold values from 0 to 30719
- query_levels: int32 [128, 32], replicated, may hold values from 1 to 255
- feedback_ids: int32 [128, 10], replicated, may hold values from 0 to 4095, as said below
Outputs:
- first_scores: float32 [128, 4096], P('term', 'doc')
- final_scores: float32 [128, 4096], P('term', 'doc')
Inputs may be any that keep to these rules, and one draw needn't show every extreme that they name: `feedback_ids`: the 1280 feedback ids are all different.
All inputs are finite; a program needn't handle non-finite values.
Results may differ from a plain program's by a relative error of at most 0.0015.
Values may be sent and summed in bfloat16 or wider, within the bound.
A program may use at most 64 MiB of HBM per device.

v0:
```python
import jax
import jax.numpy as jnp
from jax import lax
from jax.sharding import PartitionSpec as P

expansion_weight = 0.25


def query_slice(query_terms, query_levels, width, offset):
    columns = offset + lax.iota(jnp.int32, width)

    def add_term(position, total):
        ids_now = lax.dynamic_index_in_dim(query_terms, position, 1, keepdims=True)
        weight_now = (
            lax.dynamic_index_in_dim(query_levels, position, 1, keepdims=True).astype(jnp.float32)
            / 100.0
        )
        return total + jnp.where(ids_now == columns[None, :], weight_now, 0.0)

    initial = jnp.zeros((query_terms.shape[0], width), jnp.float32)
    return lax.fori_loop(0, query_terms.shape[1], add_term, initial)


def score_block(query_rows, postings):
    return lax.dot_general(
        query_rows, postings, (((1,), (1,)), ((), ())), preferred_element_type=jnp.float32
    )


def per_device(postings, query_terms, query_levels, feedback_ids):
    doc_rows, width = postings.shape
    queries = query_terms.shape[0]
    term_groups = lax.axis_size("term")
    group_rows = queries // term_groups
    term_index = lax.axis_index("term")
    doc_index = lax.axis_index("doc")
    query_part = query_slice(query_terms, query_levels, width, term_index * width)
    query_rounded = query_part.astype(jnp.bfloat16)
    local_slot = feedback_ids - doc_index * doc_rows
    positions = lax.iota(jnp.int32, doc_rows)
    selector = (local_slot[:, :, None] == positions[None, None, :]).astype(jnp.float32)
    partial_scores = score_block(query_rounded, postings)
    first_all = lax.psum(partial_scores, "term")
    first_scores = lax.dynamic_slice_in_dim(first_all, term_index * group_rows, group_rows, 0)
    feedback = jnp.sum(selector * first_all[:, None, :], axis=2).astype(jnp.bfloat16)
    feedback_wide = feedback.astype(jnp.float32)
    mixing = jnp.sum(selector * feedback_wide[:, :, None], axis=1).astype(jnp.bfloat16)
    numerator = jnp.dot(mixing, postings, preferred_element_type=jnp.float32)
    weight_part = jnp.sum(feedback_wide, axis=1)
    numerator_all, weight_sum = lax.psum((numerator, weight_part), "doc")
    expanded = (query_part + expansion_weight * numerator_all / weight_sum[:, None]).astype(
        jnp.bfloat16
    )
    final_scores = lax.psum_scatter(
        score_block(expanded, postings), "term", scatter_dimension=0, tiled=True
    )
    return (first_scores, final_scores)


def solution(mesh):
    return jax.shard_map(
        per_device,
        mesh=mesh,
        in_specs=(P("doc", "term"), P(), P(), P()),
        out_specs=(P("term", "doc"), P("term", "doc")),
        check_vma=False,
    )
```

profile of v0, /device:TPU:0, one launch (start us, length us, event | category | flops | bytes accessed | tf_op | source)
XLA Modules:
  0.0 365.7 jit_solution(14794994957368850727)
XLA Ops:
  7.2 190.6 %while.14 = (s32[]{:T(128)}, f32[128,7680]{1,0:T(8,128)}, s32[128,32]{0,1:T(8,128)}, s32[128,32]{0,1:T(8,128)}, s32[]{:T(128)}, /*index=5*/s32[]{:T(128)}, s32[]{:T(128)}) while((s32[]{:T(128)}, f32[128,7680]{1,0:T(8,128)}, s32[128,32]{0,1:T(8,128)}, s32[128,32]{0,1:T(8,128)}, s32[]{:T(128)}, /*index=5*/s32[]{:T(128)}, ...), condition=%wide.region_1.2_spmd.clone, body=%wide.region_0.1_spmd.clone.sunk | while | flops 3940099 | bytes 7928939 | solution.py:21
  7.2 0.7 multiply_bitcast_fusion.2
  8.6 2.5 select_add_fusion.2
  11.2 0.7 multiply_bitcast_fusion.2
  12.5 4.6 %select_add_fusion.2 = f32[128,7680]{1,0:T(8,128)} fusion(f32[128,7680]{1,0:T(8,128)} %get-tuple-element.167, f32[128]{0:T(128)S(1)} %multiply_bitcast_fusion.2, s32[7680]{0:T(1024)S(1)} %iota_add_fusion.2, s32[128]{0:T(128)S(1)} %dynamic-slice_bitcast_fusion.2, pred[]{:T(512)S(6)} %compare.3), kind=kLoop, calls=%fused_computation.1.clone.1 | loop fusion | flops 3932160 | bytes 7896065 | tf_op jit(solution)/shard_map/while/body/eval_jaxpr/add | solution.py:18
  17.2 0.7 multiply_bitcast_fusion.2
  18.6 4.6 %select_add_fusion.2 = f32[128,7680]{1,0:T(8,128)} fusion(f32[128,7680]{1,0:T(8,128)} %get-tuple-element.167, f32[128]{0:T(128)S(1)} %multiply_bitcast_fusion.2, s32[7680]{0:T(1024)S(1)} %iota_add_fusion.2, s32[128]{0:T(128)S(1)} %dynamic-slice_bitcast_fusion.2, pred[]{:T(512)S(6)} %compare.3), kind=kLoop, calls=%fused_computation.1.clone.1 | loop fusion | flops 3932160 | bytes 7896065 | tf_op jit(solution)/shard_map/while/body/eval_jaxpr/add | solution.py:18
  23.2 0.7 multiply_bitcast_fusion.2
  24.6 4.6 %select_add_fusion.2 = f32[128,7680]{1,0:T(8,128)} fusion(f32[128,7680]{1,0:T(8,128)} %get-tuple-element.167, f32[128]{0:T(128)S(1)} %multiply_bitcast_fusion.2, s32[7680]{0:T(1024)S(1)} %iota_add_fusion.2, s32[128]{0:T(128)S(1)} %dynamic-slice_bitcast_fusion.2, pred[]{:T(512)S(6)} %compare.3), kind=kLoop, calls=%fused_computation.1.clone.1 | loop fusion | flops 3932160 | bytes 7896065 | tf_op jit(solution)/shard_map/while/body/eval_jaxpr/add | solution.py:18
  29.2 0.7 multiply_bitcast_fusion.2
  30.6 4.6 %select_add_fusion.2 = f32[128,7680]{1,0:T(8,128)} fusion(f32[128,7680]{1,0:T(8,128)} %get-tuple-element.167, f32[128]{0:T(128)S(1)} %multiply_bitcast_fusion.2, s32[7680]{0:T(1024)S(1)} %iota_add_fusion.2, s32[128]{0:T(128)S(1)} %dynamic-slice_bitcast_fusion.2, pred[]{:T(512)S(6)} %compare.3), kind=kLoop, calls=%fused_computation.1.clone.1 | loop fusion | flops 3932160 | bytes 7896065 | tf_op jit(solution)/shard_map/while/body/eval_jaxpr/add | solution.py:18
  35.2 0.7 multiply_bitcast_fusion.2
  36.6 4.6 %select_add_fusion.2 = f32[128,7680]{1,0:T(8,128)} fusion(f32[128,7680]{1,0:T(8,128)} %get-tuple-element.167, f32[128]{0:T(128)S(1)} %multiply_bitcast_fusion.2, s32[7680]{0:T(1024)S(1)} %iota_add_fusion.2, s32[128]{0:T(128)S(1)} %dynamic-slice_bitcast_fusion.2, pred[]{:T(512)S(6)} %compare.3), kind=kLoop, calls=%fused_computation.1.clone.1 | loop fusion | flops 3932160 | bytes 7896065 | tf_op jit(solution)/shard_map/while/body/eval_jaxpr/add | solution.py:18
  42.7 4.6 %select_add_fusion.2 = f32[128,7680]{1,0:T(8,128)} fusion(f32[128,7680]{1,0:T(8,128)} %get-tuple-element.167, f32[128]{0:T(128)S(1)} %multiply_bitcast_fusion.2, s32[7680]{0:T(1024)S(1)} %iota_add_fusion.2, s32[128]{0:T(128)S(1)} %dynamic-slice_bitcast_fusion.2, pred[]{:T(512)S(6)} %compare.3), kind=kLoop, calls=%fused_computation.1.clone.1 | loop fusion | flops 3932160 | bytes 7896065 | tf_op jit(solution)/shard_map/while/body/eval_jaxpr/add | solution.py:18
  47.3 0.7 multiply_bitcast_fusion.2
  48.7 4.6 %select_add_fusion.2 = f32[128,7680]{1,0:T(8,128)} fusion(f32[128,7680]{1,0:T(8,128)} %get-tuple-element.167, f32[128]{0:T(128)S(1)} %multiply_bitcast_fusion.2, s32[7680]{0:T(1024)S(1)} %iota_add_fusion.2, s32[128]{0:T(128)S(1)} %dynamic-slice_bitcast_fusion.2, pred[]{:T(512)S(6)} %compare.3), kind=kLoop, calls=%fused_computation.1.clone.1 | loop fusion | flops 3932160 | bytes 7896065 | tf_op jit(solution)/shard_map/while/body/eval_jaxpr/add | solution.py:18
  53.3 0.7 multiply_bitcast_fusion.2
  54.7 4.6 %select_add_fusion.2 = f32[128,7680]{1,0:T(8,128)} fusion(f32[128,7680]{1,0:T(8,128)} %get-tuple-element.167, f32[128]{0:T(128)S(1)} %multiply_bitcast_fusion.2, s32[7680]{0:T(1024)S(1)} %iota_add_fusion.2, s32[128]{0:T(128)S(1)} %dynamic-slice_bitcast_fusion.2, pred[]{:T(512)S(6)} %compare.3), kind=kLoop, calls=%fused_computation.1.clone.1 | loop fusion | flops 3932160 | bytes 7896065 | tf_op jit(solution)/shard_map/while/body/eval_jaxpr/add | solution.py:18
  59.3 0.7 multiply_bitcast_fusion.2
  60.7 4.6 %select_add_fusion.2 = f32[128,7680]{1,0:T(8,128)} fusion(f32[128,7680]{1,0:T(8,128)} %get-tuple-element.167, f32[128]{0:T(128)S(1)} %multiply_bitcast_fusion.2, s32[7680]{0:T(1024)S(1)} %iota_add_fusion.2, s32[128]{0:T(128)S(1)} %dynamic-slice_bitcast_fusion.2, pred[]{:T(512)S(6)} %compare.3), kind=kLoop, calls=%fused_computation.1.clone.1 | loop fusion | flops 3932160 | bytes 7896065 | tf_op jit(solution)/shard_map/while/body/eval_jaxpr/add | solution.py:18
  65.3 0.7 multiply_bitcast_fusion.2
  66.7 4.6 %select_add_fusion.2 = f32[128,7680]{1,0:T(8,128)} fusion(f32[128,7680]{1,0:T(8,128)} %get-tuple-element.167, f32[128]{0:T(128)S(1)} %multiply_bitcast_fusion.2, s32[7680]{0:T(1024)S(1)} %iota_add_fusion.2, s32[128]{0:T(128)S(1)} %dynamic-slice_bitcast_fusion.2, pred[]{:T(512)S(6)} %compare.3), kind=kLoop, calls=%fused_computation.1.clone.1 | loop fusion | flops 3932160 | bytes 7896065 | tf_op jit(solution)/shard_map/while/body/eval_jaxpr/add | solution.py:18
  71.4 0.7 multiply_bitcast_fusion.2
  72.8 4.6 %select_add_fusion.2 = f32[128,7680]{1,0:T(8,128)} fusion(f32[128,7680]{1,0:T(8,128)} %get-tuple-element.167, f32[128]{0:T(128)S(1)} %multiply_bitcast_fusion.2, s32[7680]{0:T(1024)S(1)} %iota_add_fusion.2, s32[128]{0:T(128)S(1)} %dynamic-slice_bitcast_fusion.2, pred[]{:T(512)S(6)} %compare.3), kind=kLoop, calls=%fused_computation.1.clone.1 | loop fusion | flops 3932160 | bytes 7896065 | tf_op jit(solution)/shard_map/while/body/eval_jaxpr/add | solution.py:18
  77.4 0.7 multiply_bitcast_fusion.2
  78.8 4.6 %select_add_fusion.2 = f32[128,7680]{1,0:T(8,128)} fusion(f32[128,7680]{1,0:T(8,128)} %get-tuple-element.167, f32[128]{0:T(128)S(1)} %multiply_bitcast_fusion.2, s32[7680]{0:T(1024)S(1)} %iota_add_fusion.2, s32[128]{0:T(128)S(1)} %dynamic-slice_bitcast_fusion.2, pred[]{:T(512)S(6)} %compare.3), kind=kLoop, calls=%fused_computation.1.clone.1 | loop fusion | flops 3932160 | bytes 7896065 | tf_op jit(solution)/shard_map/while/body/eval_jaxpr/add | solution.py:18
  83.4 0.7 multiply_bitcast_fusion.2
  84.8 4.6 %select_add_fusion.2 = f32[128,7680]{1,0:T(8,128)} fusion(f32[128,7680]{1,0:T(8,128)} %get-tuple-element.167, f32[128]{0:T(128)S(1)} %multiply_bitcast_fusion.2, s32[7680]{0:T(1024)S(1)} %iota_add_fusion.2, s32[128]{0:T(128)S(1)} %dynamic-slice_bitcast_fusion.2, pred[]{:T(512)S(6)} %compare.3), kind=kLoop, calls=%fused_computation.1.clone.1 | loop fusion | flops 3932160 | bytes 7896065 | tf_op jit(solution)/shard_map/while/body/eval_jaxpr/add | solution.py:18
  90.8 4.6 %select_add_fusion.2 = f32[128,7680]{1,0:T(8,128)} fusion(f32[128,7680]{1,0:T(8,128)} %get-tuple-element.167, f32[128]{0:T(128)S(1)} %multiply_bitcast_fusion.2, s32[7680]{0:T(1024)S(1)} %iota_add_fusion.2, s32[128]{0:T(128)S(1)} %dynamic-slice_bitcast_fusion.2, pred[]{:T(512)S(6)} %compare.3), kind=kLoop, calls=%fused_computation.1.clone.1 | loop fusion | flops 3932160 | bytes 7896065 | tf_op jit(solution)/shard_map/while/body/eval_jaxpr/add | solution.py:18
  95.5 0.7 multiply_bitcast_fusion.2
  96.8 4.6 %select_add_fusion.2 = f32[128,7680]{1,0:T(8,128)} fusion(f32[128,7680]{1,0:T(8,128)} %get-tuple-element.167, f32[128]{0:T(128)S(1)} %multiply_bitcast_fusion.2, s32[7680]{0:T(1024)S(1)} %iota_add_fusion.2, s32[128]{0:T(128)S(1)} %dynamic-slice_bitcast_fusion.2, pred[]{:T(512)S(6)} %compare.3), kind=kLoop, calls=%fused_computation.1.clone.1 | loop fusion | flops 3932160 | bytes 7896065 | tf_op jit(solution)/shard_map/while/body/eval_jaxpr/add | solution.py:18
  101.5 0.7 multiply_bitcast_fusion.2
  102.9 4.6 %select_add_fusion.2 = f32[128,7680]{1,0:T(8,128)} fusion(f32[128,7680]{1,0:T(8,128)} %get-tuple-element.167, f32[128]{0:T(128)S(1)} %multiply_bitcast_fusion.2, s32[7680]{0:T(1024)S(1)} %iota_add_fusion.2, s32[128]{0:T(128)S(1)} %dynamic-slice_bitcast_fusion.2, pred[]{:T(512)S(6)} %compare.3), kind=kLoop, calls=%fused_computation.1.clone.1 | loop fusion | flops 3932160 | bytes 7896065 | tf_op jit(solution)/shard_map/while/body/eval_jaxpr/add | solution.py:18
  107.5 0.7 multiply_bitcast_fusion.2
  108.9 4.6 %select_add_fusion.2 = f32[128,7680]{1,0:T(8,128)} fusion(f32[128,7680]{1,0:T(8,128)} %get-tuple-element.167, f32[128]{0:T(128)S(1)} %multiply_bitcast_fusion.2, s32[7680]{0:T(1024)S(1)} %iota_add_fusion.2, s32[128]{0:T(128)S(1)} %dynamic-slice_bitcast_fusion.2, pred[]{:T(512)S(6)} %compare.3), kind=kLoop, calls=%fused_computation.1.clone.1 | loop fusion | flops 3932160 | bytes 7896065 | tf_op jit(solution)/shard_map/while/body/eval_jaxpr/add | solution.py:18
  113.5 0.7 multiply_bitcast_fusion.2
  114.9 4.6 %select_add_fusion.2 = f32[128,7680]{1,0:T(8,128)} fusion(f32[128,7680]{1,0:T(8,128)} %get-tuple-element.167, f32[128]{0:T(128)S(1)} %multiply_bitcast_fusion.2, s32[7680]{0:T(1024)S(1)} %iota_add_fusion.2, s32[128]{0:T(128)S(1)} %dynamic-slice_bitcast_fusion.2, pred[]{:T(512)S(6)} %compare.3), kind=kLoop, calls=%fused_computation.1.clone.1 | loop fusion | flops 3932160 | bytes 7896065 | tf_op jit(solution)/shard_map/while/body/eval_jaxpr/add | solution.py:18
  119.5 0.7 multiply_bitcast_fusion.2
  120.9 4.6 %select_add_fusion.2 = f32[128,7680]{1,0:T(8,128)} fusion(f32[128,7680]{1,0:T(8,128)} %get-tuple-element.167, f32[128]{0:T(128)S(1)} %multiply_bitcast_fusion.2, s32[7680]{0:T(1024)S(1)} %iota_add_fusion.2, s32[128]{0:T(128)S(1)} %dynamic-slice_bitcast_fusion.2, pred[]{:T(512)S(6)} %compare.3), kind=kLoop, calls=%fused_computation.1.clone.1 | loop fusion | flops 3932160 | bytes 7896065 | tf_op jit(solution)/shard_map/while/body/eval_jaxpr/add | solution.py:18
  125.6 0.7 multiply_bitcast_fusion.2
  126.9 4.6 %select_add_fusion.2 = f32[128,7680]{1,0:T(8,128)} fusion(f32[128,7680]{1,0:T(8,128)} %get-tuple-element.167, f32[128]{0:T(128)S(1)} %multiply_bitcast_fusion.2, s32[7680]{0:T(1024)S(1)} %iota_add_fusion.2, s32[128]{0:T(128)S(1)} %dynamic-slice_bitcast_fusion.2, pred[]{:T(512)S(6)} %compare.3), kind=kLoop, calls=%fused_computation.1.clone.1 | loop fusion | flops 3932160 | bytes 7896065 | tf_op jit(solution)/shard_map/while/body/eval_jaxpr/add | solution.py:18
  131.6 0.7 multiply_bitcast_fusion.2
  133.0 4.6 %select_add_fusion.2 = f32[128,7680]{1,0:T(8,128)} fusion(f32[128,7680]{1,0:T(8,128)} %get-tuple-element.167, f32[128]{0:T(128)S(1)} %multiply_bitcast_fusion.2, s32[7680]{0:T(1024)S(1)} %iota_add_fusion.2, s32[128]{0:T(128)S(1)} %dynamic-slice_bitcast_fusion.2, pred[]{:T(512)S(6)} %compare.3), kind=kLoop, calls=%fused_computation.1.clone.1 | loop fusion | flops 3932160 | bytes 7896065 | tf_op jit(solution)/shard_map/while/body/eval_jaxpr/add | solution.py:18
  137.6 0.7 multiply_bitcast_fusion.2
  139.0 4.6 %select_add_fusion.2 = f32[128,7680]{1,0:T(8,128)} fusion(f32[128,7680]{1,0:T(8,128)} %get-tuple-element.167, f32[128]{0:T(128)S(1)} %multiply_bitcast_fusion.2, s32[7680]{0:T(1024)S(1)} %iota_add_fusion.2, s32[128]{0:T(128)S(1)} %dynamic-slice_bitcast_fusion.2, pred[]{:T(512)S(6)} %compare.3), kind=kLoop, calls=%fused_computation.1.clone.1 | loop fusion | flops 3932160 | bytes 7896065 | tf_op jit(solution)/shard_map/while/body/eval_jaxpr/add | solution.py:18
  143.6 0.7 multiply_bitcast_fusion.2
  145.0 4.6 %select_add_fusion.2 = f32[128,7680]{1,0:T(8,128)} fusion(f32[128,7680]{1,0:T(8,128)} %get-tuple-element.167, f32[128]{0:T(128)S(1)} %multiply_bitcast_fusion.2, s32[7680]{0:T(1024)S(1)} %iota_add_fusion.2, s32[128]{0:T(128)S(1)} %dynamic-slice_bitcast_fusion.2, pred[]{:T(512)S(6)} %compare.3), kind=kLoop, calls=%fused_computation.1.clone.1 | loop fusion | flops 3932160 | bytes 7896065 | tf_op jit(solution)/shard_map/while/body/eval_jaxpr/add | solution.py:18
  151.0 4.6 %select_add_fusion.2 = f32[128,7680]{1,0:T(8,128)} fusion(f32[128,7680]{1,0:T(8,128)} %get-tuple-element.167, f32[128]{0:T(128)S(1)} %multiply_bitcast_fusion.2, s32[7680]{0:T(1024)S(1)} %iota_add_fusion.2, s32[128]{0:T(128)S(1)} %dynamic-slice_bitcast_fusion.2, pred[]{:T(512)S(6)} %compare.3), kind=kLoop, calls=%fused_computation.1.clone.1 | loop fusion | flops 3932160 | bytes 7896065 | tf_op jit(solution)/shard_map/while/body/eval_jaxpr/add | solution.py:18
  157.1 4.6 %select_add_fusion.2 = f32[128,7680]{1,0:T(8,128)} fusion(f32[128,7680]{1,0:T(8,128)} %get-tuple-element.167, f32[128]{0:T(128)S(1)} %multiply_bitcast_fusion.2, s32[7680]{0:T(1024)S(1)} %iota_add_fusion.2, s32[128]{0:T(128)S(1)} %dynamic-slice_bitcast_fusion.2, pred[]{:T(512)S(6)} %compare.3), kind=kLoop, calls=%fused_computation.1.clone.1 | loop fusion | flops 3932160 | bytes 7896065 | tf_op jit(solution)/shard_map/while/body/eval_jaxpr/add | solution.py:18
  163.1 4.6 %select_add_fusion.2 = f32[128,7680]{1,0:T(8,128)} fusion(f32[128,7680]{1,0:T(8,128)} %get-tuple-element.167, f32[128]{0:T(128)S(1)} %multiply_bitcast_fusion.2, s32[7680]{0:T(1024)S(1)} %iota_add_fusion.2, s32[128]{0:T(128)S(1)} %dynamic-slice_bitcast_fusion.2, pred[]{:T(512)S(6)} %compare.3), kind=kLoop, calls=%fused_computation.1.clone.1 | loop fusion | flops 3932160 | bytes 7896065 | tf_op jit(solution)/shard_map/while/body/eval_jaxpr/add | solution.py:18
  169.1 4.6 %select_add_fusion.2 = f32[128,7680]{1,0:T(8,128)} fusion(f32[128,7680]{1,0:T(8,128)} %get-tuple-element.167, f32[128]{0:T(128)S(1)} %multiply_bitcast_fusion.2, s32[7680]{0:T(1024)S(1)} %iota_add_fusion.2, s32[128]{0:T(128)S(1)} %dynamic-slice_bitcast_fusion.2, pred[]{:T(512)S(6)} %compare.3), kind=kLoop, calls=%fused_computation.1.clone.1 | loop fusion | flops 3932160 | bytes 7896065 | tf_op jit(solution)/shard_map/while/body/eval_jaxpr/add | solution.py:18
  175.1 4.6 %select_add_fusion.2 = f32[128,7680]{1,0:T(8,128)} fusion(f32[128,7680]{1,0:T(8,128)} %get-tuple-element.167, f32[128]{0:T(128)S(1)} %multiply_bitcast_fusion.2, s32[7680]{0:T(1024)S(1)} %iota_add_fusion.2, s32[128]{0:T(128)S(1)} %dynamic-slice_bitcast_fusion.2, pred[]{:T(512)S(6)} %compare.3), kind=kLoop, calls=%fused_computation.1.clone.1 | loop fusion | flops 3932160 | bytes 7896065 | tf_op jit(solution)/shard_map/while/body/eval_jaxpr/add | solution.py:18
  181.1 4.6 %select_add_fusion.2 = f32[128,7680]{1,0:T(8,128)} fusion(f32[128,7680]{1,0:T(8,128)} %get-tuple-element.167, f32[128]{0:T(128)S(1)} %multiply_bitcast_fusion.2, s32[7680]{0:T(1024)S(1)} %iota_add_fusion.2, s32[128]{0:T(128)S(1)} %dynamic-slice_bitcast_fusion.2, pred[]{:T(512)S(6)} %compare.3), kind=kLoop, calls=%fused_computation.1.clone.1 | loop fusion | flops 3932160 | bytes 7896065 | tf_op jit(solution)/shard_map/while/body/eval_jaxpr/add | solution.py:18
  187.2 4.6 %select_add_fusion.2 = f32[128,7680]{1,0:T(8,128)} fusion(f32[128,7680]{1,0:T(8,128)} %get-tuple-element.167, f32[128]{0:T(128)S(1)} %multiply_bitcast_fusion.2, s32[7680]{0:T(1024)S(1)} %iota_add_fusion.2, s32[128]{0:T(128)S(1)} %dynamic-slice_bitcast_fusion.2, pred[]{:T(512)S(6)} %compare.3), kind=kLoop, calls=%fused_computation.1.clone.1 | loop fusion | flops 3932160 | bytes 7896065 | tf_op jit(solution)/shard_map/while/body/eval_jaxpr/add | solution.py:18
  193.2 4.6 %select_add_fusion.2 = f32[128,7680]{1,0:T(8,128)} fusion(f32[128,7680]{1,0:T(8,128)} %get-tuple-element.167, f32[128]{0:T(128)S(1)} %multiply_bitcast_fusion.2, s32[7680]{0:T(1024)S(1)} %iota_add_fusion.2, s32[128]{0:T(128)S(1)} %dynamic-slice_bitcast_fusion.2, pred[]{:T(512)S(6)} %compare.3), kind=kLoop, calls=%fused_computation.1.clone.1 | loop fusion | flops 3932160 | bytes 7896065 | tf_op jit(solution)/shard_map/while/body/eval_jaxpr/add | solution.py:18
  197.8 7.8 %fusion.2 = f32[128,512]{1,0:T(8,128)} fusion(bf16[512,7680]{1,0:T(8,128)(2,1)} %param.6, f32[128,7680]{1,0:T(8,128)} %get-tuple-element.96), kind=kOutput, calls=%fused_computation.9 | convolution fusion | flops 1007616000 | bytes 12058624 | tf_op jit(solution)/shard_map/dot_general | solution.py:25
  205.7 38.1 %all-reduce.3.cloned.1.call-done = f32[128,512]{1,0:T(8,128)} async-done(((f32[128,512]{1,0:T(8,128)}), f32[128,512]{1,0:T(8,128)}) %all-reduce.3.cloned.1.call-update) | async-done | bytes 262160 | tf_op jit(solution)/shard_map/psum | solution.py:43
  243.8 1.5 select_reduce_fusion.1
  245.8 6.5 %fusion.9 = f32[128,7680]{1,0:T(8,128)} fusion(bf16[128,512]{1,0:T(8,128)(2,1)S(1)} %select_reduce_fusion, bf16[512,7680]{1,0:T(8,128)(2,1)} %param.6), kind=kOutput, calls=%fused_computation.19 | convolution fusion | flops 1006632960 | bytes 11927552 | tf_op jit(solution)/shard_map/dot_general | solution.py:48
  252.3 12.4 %psum.23 = f32[128]{0:T(128)S(1)} all-reduce(f32[128]{0:T(128)S(1)} %fusion.7), channel_id=1, replica_groups=mesh['term'=4,'doc'=8] {'doc'}, use_global_device_ids=true, to_apply=%region_7.8 | all-reduce | flops 128 | bytes 1024 | tf_op jit(solution)/shard_map/psum | solution.py:50
  264.7 65.6 %all-reduce.5.cloned.1.call-done = f32[128,7680]{1,0:T(8,128)} async-done(((f32[128,7680]{1,0:T(8,128)}), f32[128,7680]{1,0:T(8,128)}) %all-reduce.5.cloned.1.call-update) | async-done | bytes 3932176 | tf_op jit(solution)/shard_map/psum | solution.py:50
  330.3 9.0 %fusion.4 = f32[128,512]{1,0:T(8,128)} fusion(bf16[512,7680]{1,0:T(8,128)(2,1)} %param.6, f32[128,7680]{1,0:T(8,128)} %get-tuple-element.96, f32[128,7680]{1,0:T(8,128)} %all-reduce.5.cloned.1.call-done, f32[128]{0:T(128)S(1)} %psum.23), kind=kOutput, calls=%fused_computation.11 | convolution fusion | flops 1010565120 | bytes 15991296 | tf_op jit(solution)/shard_map/dot_general | solution.py:25
  339.3 1.5 constant_dynamic-slice_fusion
  340.8 18.4 %reduce-scatter.2.cloned.1.call-done = f32[32,512]{1,0:T(8,128)} async-done(((f32[128,512]{1,0:T(8,128)}), f32[32,512]{1,0:T(8,128)}) %reduce-scatter.2.cloned.1.call-update) | async-done | bytes 65552 | tf_op jit(solution)/shard_map/reduce_scatter | solution.py:54
  (87 shorter events, 29.8 us)
Async XLA Ops:
  7.2 236.6 %all-reduce.3.cloned.1.call-start = ((), (), s32[]{:S(2)}) async-start(), calls=%async_computation.1 | async-start | bytes 524288 | tf_op jit(solution)/shard_map/psum | solution.py:43
  197.8 7.9 %copy-start = (s32[128,10]{0,1:T(8,128)S(1)}, s32[128,10]{0,1:T(8,128)}, u32[]{:S(2)}) copy-start(s32[128,10]{0,1:T(8,128)} %param.9) | copy-start | bytes 15364
  205.6 124.7 %all-reduce.5.cloned.1.call-start = ((), (), s32[]{:S(2)}) async-start(), calls=%async_computation.2 | async-start | bytes 7864320 | tf_op jit(solution)/shard_map/psum | solution.py:50
  252.2 106.9 %reduce-scatter.2.cloned.1.call-start = ((), (), s32[]{:S(2)}) async-start(), calls=%async_computation.3 | async-start | bytes 327680 | tf_op jit(solution)/shard_map/reduce_scatter | solution.py:54
Sparse Core Ops, SparseCore 0:
  205.8 37.9 all-reduce.2
  252.3 77.8 all-reduce.4
  339.4 19.7 reduce-scatter.1
where the time goes:
time: 369 us; the launch traced here: 366 us
  other arithmetic  170 us (46%)
  waiting for transfers between devices  122 us (33%)
  local copies, waits for them, and re-layouts  23.6 us (6%)
  matrix products  23.2 us (6%)
  between operations  13.8 us (4%)
  blocking collectives  12.4 us (3%)
    add x32, other arithmetic, add_term(): return total + jnp.where(ids_now == columns[None, :], weight_now, 0.0)  146 us
    psum x1, waiting for transfers between devices, per_device(): numerator_all, weight_sum = lax.psum((numerator, weight_part), 'doc')  65.6 us
    psum x1, waiting for transfers between devices, per_device(): first_all = lax.psum(partial_scores, 'term')  38.1 us
    broadcast_in_dim x32, other arithmetic, add_term(): return total + jnp.where(ids_now == columns[None, :], weight_now, 0.0)  22.2 us
    eq x32, local copies, waits for them, and re-layouts, add_term(): return total + jnp.where(ids_now == columns[None, :], weight_now, 0.0)  22.1 us
    reduce_scatter x1, waiting for transfers between devices, per_device(): lax.psum_scatter(score_block(expanded, postings), 'term', scatter_dimensi...  18.4 us
    dot_general x2, matrix products, score_block(): lax.dot_general(query_rows, postings, (((1,), (1,)), ((), ())), preferred...  16.8 us
    psum x1, blocking collectives, per_device(): numerator_all, weight_sum = lax.psum((numerator, weight_part), 'doc')  12.4 us
  transfers between devices with their start and end apart: 3, of which 3 were waited for; matrix products, arithmetic and copies ran while one was open for 0% of the time, Pallas kernels for 0%

commit v1 on v0

v1 whole, which is shorter than its diff:
```python
import functools

import jax
import jax.numpy as jnp
from jax import lax
from jax.experimental import pallas as pl
from jax.experimental.pallas import tpu as pltpu
from jax.sharding import PartitionSpec as P

expansion_weight = 0.25
MESH = pl.DeviceIdType.MESH
LANES = 128
NT = (((1,), (1,)), ((), ()))
f32 = jnp.float32
bf16 = jnp.bfloat16


def dot_nt(a, b):
    return lax.dot_general(a, b, NT, preferred_element_type=f32)


def fused_kernel(
    n_term, n_doc, chunks,
    postings, terms, levels, ids, first_out, final_out,
    p_ref, q_ref, hi_ref, lo_ref, lev_ref, part_ref, sel_ref, mix_ref,
    fb_ref, first_ref, ws_ref, wcol_ref, nb_ref, tw_ref, s1_ref, a_ref, s2_ref, b_ref,
    e_ref, acc_ref, last_ref,
    p_sem, fb_send, fb_recv, first_send, first_recv, ws_send, ws_recv,
    pipe_send, pipe_recv, last_send, last_recv,
):
    t = lax.axis_index("term")
    d = lax.axis_index("doc")
    docs, width = p_ref.shape
    queries, slots = terms.shape
    cw = width // chunks
    his = width // LANES
    rows_out = queries // n_term
    half, quarter, eighth = queries // 2, queries // 4, queries // 8

    core = d % 2
    bit1 = (d // 2) % 2
    bit2 = (d // 4) % 2

    def cols(c):
        return pl.ds(pl.multiple_of(c * cw, LANES), cw)

    def load(c):
        return pltpu.make_async_copy(postings.at[:, cols(c)], p_ref.at[:, cols(c)], p_sem.at[c])

    for c in range(chunks):
        load(c).start()

    barrier = pltpu.get_barrier_semaphore()
    for o in range(1, n_term):
        pl.semaphore_signal(barrier, inc=1, device_id={"term": (t + o) % n_term}, device_id_type=MESH)
    for o in range(1, n_doc):
        pl.semaphore_signal(barrier, inc=1, device_id={"doc": (d + o) % n_doc}, device_id_type=MESH)

    group = 8 * slots
    spread = (
        lax.broadcasted_iota(jnp.int32, (slots, group), 0)
        == lax.broadcasted_iota(jnp.int32, (slots, group), 1) % slots
    ).astype(bf16)
    own = (
        lax.broadcasted_iota(jnp.int32, (queries, group), 0) % 8
        == lax.broadcasted_iota(jnp.int32, (queries, group), 1) // slots
    )

    def lay(values):
        wide = jnp.dot(values.astype(f32).astype(bf16), spread, preferred_element_type=f32)
        return jnp.sum(jnp.where(own, wide, 0.0).reshape(queries // 8, 8, group), axis=1)

    ids_now = terms[...]
    q8 = (lax.broadcasted_iota(jnp.int32, (queries // 8, group), 1) // slots).astype(f32)
    hi = lay(ids_now // LANES) - (t * his).astype(f32)
    hi_ref[...] = hi * 8.0 + q8
    lo_ref[...] = lay(ids_now % LANES)
    lev_ref[...] = lay(levels[...])

    row_code = lax.broadcasted_iota(jnp.int32, (his * 8, group), 0).astype(f32)
    lane_code = lax.broadcasted_iota(jnp.int32, (LANES, group), 0).astype(f32)

    def build(g, carry):
        left = jnp.where(
            hi_ref[pl.ds(g, 1), :] == row_code, lev_ref[pl.ds(g, 1), :], 0.0
        ).astype(bf16)
        right = jnp.where(lo_ref[pl.ds(g, 1), :] == lane_code, 1.0, 0.0).astype(bf16)
        block = dot_nt(left, right) * 0.01
        rows = pl.ds(pl.multiple_of(g * 8, 8), 8)
        for h in range(his):
            q_ref[rows, h * LANES : (h + 1) * LANES] = block[h * 8 : (h + 1) * 8]
        return carry

    lax.fori_loop(0, queries // 8, build, 0)

    place = lax.broadcasted_iota(jnp.int32, (queries, docs), 1)
    local = ids[...] - d * docs
    sel = place == local[:, 0:1]
    for j in range(1, local.shape[1]):
        sel = sel | (place == local[:, j : j + 1])
    sel_ref[...] = jnp.where(sel, 1.0, 0.0)

    part_ref[...] = jnp.zeros_like(part_ref)

    def score(c, carry):
        load(c).wait()
        part_ref[...] += dot_nt(q_ref[:, cols(c)].astype(bf16), p_ref[:, cols(c)])
        return carry

    lax.fori_loop(0, chunks, score, 0)

    pl.semaphore_wait(barrier, n_term + n_doc - 2)

    fb_ref[t] = jnp.sum((sel_ref[...] * part_ref[...]).reshape(queries // 8, 8, docs), axis=0)

    def fb_copy(o):
        return pltpu.make_async_remote_copy(
            fb_ref.at[t], fb_ref.at[t], fb_send.at[o - 1], fb_recv.at[o - 1],
            device_id={"term": (t + o) % n_term}, device_id_type=MESH,
        )

    def first_copy(o):
        peer = (t + o) % n_term
        return pltpu.make_async_remote_copy(
            part_ref.at[pl.ds(pl.multiple_of(peer * rows_out, 8), rows_out), :], first_ref.at[t],
            first_send.at[o - 1], first_recv.at[o - 1],
            device_id={"term": peer}, device_id_type=MESH,
        )

    def last_copy(o):
        peer = (t + o) % n_term
        return pltpu.make_async_remote_copy(
            acc_ref.at[pl.ds(pl.multiple_of(peer * rows_out, 8), rows_out), :], last_ref.at[t],
            last_send.at[o - 1], last_recv.at[o - 1],
            device_id={"term": peer}, device_id_type=MESH,
        )

    def ws_copy(o):
        return pltpu.make_async_remote_copy(
            ws_ref.at[d], ws_ref.at[d], ws_send.at[o - 1], ws_recv.at[o - 1],
            device_id={"doc": (d + o) % n_doc}, device_id_type=MESH,
        )

    for o in range(1, n_term):
        fb_copy(o).start()
    for o in range(1, n_term):
        first_copy(o).start()
    own_rows = pl.ds(pl.multiple_of(t * rows_out, 8), rows_out)
    first_ref[t] = part_ref[own_rows, :]
    for o in range(1, n_term):
        fb_copy(o).wait_recv()
    fb_sum = fb_ref[0]
    for s in range(1, n_term):
        fb_sum = fb_sum + fb_ref[s]
    fb_row = jnp.sum(fb_sum, axis=0, keepdims=True)
    mix_ref[...] = (sel_ref[...] * fb_row).astype(bf16)

    ones = jnp.ones((16, docs), bf16)
    ws_ref[d] = dot_nt(ones, mix_ref[...])[:8]
    for o in range(1, n_doc):
        ws_copy(o).start()

    def copy_of(step, c, src, dst, peer):
        return pltpu.make_async_remote_copy(
            src, dst, pipe_send.at[step, c], pipe_recv.at[step, c],
            device_id={"doc": peer}, device_id_type=MESH,
        )

    twin = d + 1 - 2 * core

    def way(c):
        odd = c % 2
        even = 1 - odd
        in1 = even * bit1 + odd * bit2
        in2 = even * bit2 + odd * bit1
        peer1 = d + (even * 2 + odd * 4) * (1 - 2 * in1)
        peer2 = d + (even * 4 + odd * 2) * (1 - 2 * in2)
        return in1, in2, peer1, peer2

    def rows(start, size):
        return pl.ds(pl.multiple_of(start, 16), size)

    def exchange(step, c):
        in1, in2, peer1, peer2 = way(c)
        here = cols(c)
        if step == 0:
            return copy_of(0, c, nb_ref.at[rows((1 - core) * half, half), here], tw_ref.at[:, here], twin)
        if step == 1:
            return copy_of(1, c, s1_ref.at[rows((1 - in1) * quarter, quarter), here], a_ref.at[:, here], peer1)
        if step == 2:
            return copy_of(2, c, s2_ref.at[rows((1 - in2) * eighth, eighth), here], b_ref.at[:, here], peer2)
        base = core * half
        if step == 3:
            at = e_ref.at[rows(base + in1 * quarter + in2 * eighth, eighth), here]
            return copy_of(3, c, at, at, peer2)
        if step == 4:
            at = e_ref.at[rows(base + in1 * quarter, quarter), here]
            return copy_of(4, c, at, at, peer1)
        at = e_ref.at[rows(base, half), here]
        return copy_of(5, c, at, at, twin)

    acc_ref[...] = jnp.zeros_like(acc_ref)

    def stage(step, s, body):
        c = s - step

        @pl.when((c >= 0) & (c < chunks))
        def _():
            body(c)

    def step1(c):
        exchange(0, c).wait_recv()
        here = cols(c)
        s1_ref[:, here] = (
            nb_ref[rows(core * half, half), here].astype(f32) + tw_ref[:, here].astype(f32)
        ).astype(bf16)
        exchange(1, c).start()

    def step2(c):
        in1, in2, _, _ = way(c)
        exchange(1, c).wait_recv()
        here = cols(c)
        s2_ref[:, here] = (
            s1_ref[rows(in1 * quarter, quarter), here].astype(f32) + a_ref[:, here].astype(f32)
        ).astype(bf16)
        exchange(2, c).start()

    def step3(c):
        in1, in2, _, _ = way(c)
        exchange(2, c).wait_recv()
        here = cols(c)
        numerator = s2_ref[rows(in2 * eighth, eighth), here].astype(f32) + b_ref[:, here].astype(f32)
        mine = rows(core * half + in1 * quarter + in2 * eighth, eighth)
        total = wcol_ref[mine, :][:, 0:1]
        e_ref[mine, here] = (q_ref[mine, here] + expansion_weight * numerator / total).astype(bf16)
        exchange(3, c).start()

    def step4(c):
        exchange(3, c).wait_recv()
        exchange(4, c).start()

    def step5(c):
        exchange(4, c).wait_recv()
        exchange(5, c).start()

    def step0(c):
        here = cols(c)
        nb_ref[:, here] = jnp.dot(mix_ref[...], p_ref[:, here], preferred_element_type=f32).astype(bf16)
        exchange(0, c).start()

    def step6(c):
        exchange(5, c).wait_recv()
        here = cols(c)
        acc_ref[...] += dot_nt(e_ref[:, here], p_ref[:, here])

    def pipeline(s, carry):
        @pl.when(s == 3)
        def _():
            for o in range(1, n_doc):
                ws_copy(o).wait_recv()
            total = ws_ref[0]
            for o in range(1, n_doc):
                total = total + ws_ref[o]
            shape = (queries, queries)
            eye = lax.broadcasted_iota(jnp.int32, shape, 0) == lax.broadcasted_iota(jnp.int32, shape, 1)
            column = jnp.sum(jnp.where(eye, total[0:1, :], 0.0), axis=1, keepdims=True)
            wcol_ref[...] = jnp.broadcast_to(column, wcol_ref.shape)

        stage(5, s, step5)
        stage(4, s, step4)
        stage(3, s, step3)
        stage(2, s, step2)
        stage(1, s, step1)
        stage(0, s, step0)
        stage(6, s, step6)
        return carry

    lax.fori_loop(0, chunks + 6, pipeline, 0)

    for o in range(1, n_term):
        last_copy(o).start()

    for o in range(1, n_term):
        first_copy(o).wait_recv()
    total = first_ref[0]
    for s in range(1, n_term):
        total = total + first_ref[s]
    first_out[...] = total

    last_ref[t] = acc_ref[own_rows, :]
    for o in range(1, n_term):
        last_copy(o).wait_recv()
    total = last_ref[0]
    for s in range(1, n_term):
        total = total + last_ref[s]
    final_out[...] = total

    for o in range(1, n_term):
        fb_copy(o).wait_send()
        first_copy(o).wait_send()
        last_copy(o).wait_send()
    for o in range(1, n_doc):
        ws_copy(o).wait_send()

    def drain(c, carry):
        for step in range(6):
            exchange(step, c).wait_send()
        return carry

    lax.fori_loop(0, chunks, drain, 0)


def fused(postings, query_terms, query_levels, feedback_ids):
    docs, width = postings.shape
    queries, slots = query_terms.shape
    n_term, n_doc = lax.axis_size("term"), lax.axis_size("doc")
    chunks = next(c for c in (6, 4, 2, 1) if width % (c * LANES) == 0)
    rows_out = queries // n_term
    group = 8 * slots
    vmem = pltpu.VMEM
    dma = pltpu.SemaphoreType.DMA
    out = jax.ShapeDtypeStruct((rows_out, docs), f32)
    return pl.pallas_call(
        functools.partial(fused_kernel, n_term, n_doc, chunks),
        out_shape=(out, out),
        in_specs=[pl.BlockSpec(memory_space=pl.ANY)] + [pl.BlockSpec(memory_space=pltpu.VMEM)] * 3,
        out_specs=(pl.BlockSpec(memory_space=pltpu.VMEM),) * 2,
        scratch_shapes=[
            vmem((docs, width), bf16),
            vmem((queries, width), f32),
            vmem((queries // 8, group), f32),
            vmem((queries // 8, group), f32),
            vmem((queries // 8, group), f32),
            vmem((queries, docs), f32),
            vmem((queries, docs), f32),
            vmem((queries, docs), bf16),
            vmem((n_term, 8, docs), f32),
            vmem((n_term, rows_out, docs), f32),
            vmem((n_doc, 8, queries), f32),
            vmem((queries, LANES), f32),
            vmem((queries, width), bf16),
            vmem((queries // 2, width), bf16),
            vmem((queries // 2, width), bf16),
            vmem((queries // 4, width), bf16),
            vmem((queries // 4, width), bf16),
            vmem((queries // 8, width), bf16),
            vmem((queries, width), bf16),
            vmem((queries, docs), f32),
            vmem((n_term, rows_out, docs), f32),
            dma((chunks,)),
            dma((n_term - 1,)),
            dma((n_term - 1,)),
            dma((n_term - 1,)),
            dma((n_term - 1,)),
            dma((n_doc - 1,)),
            dma((n_doc - 1,)),
            dma((6, chunks)),
            dma((6, chunks)),
            dma((n_term - 1,)),
            dma((n_term - 1,)),
        ],
        compiler_params=pltpu.CompilerParams(
            collective_id=0, has_side_effects=True, vmem_limit_bytes=48 * 1024 * 1024
        ),
        cost_estimate=pl.CostEstimate(
            flops=6 * queries * docs * width, bytes_accessed=2 * docs * width, transcendentals=0
        ),
        name="fused_feedback",
    )(postings, query_terms, query_levels, feedback_ids)


def query_slice(query_terms, query_levels, width, offset):
    columns = offset + lax.iota(jnp.int32, width)

    def add_term(position, total):
        ids_now = lax.dynamic_index_in_dim(query_terms, position, 1, keepdims=True)
        weight_now = (
            lax.dynamic_index_in_dim(query_levels, position, 1, keepdims=True).astype(f32) / 100.0
        )
        return total + jnp.where(ids_now == columns[None, :], weight_now, 0.0)

    initial = jnp.zeros((query_terms.shape[0], width), f32)
    return lax.fori_loop(0, query_terms.shape[1], add_term, initial)


def general(postings, query_terms, query_levels, feedback_ids):
    doc_rows, width = postings.shape
    queries = query_terms.shape[0]
    group_rows = queries // lax.axis_size("term")
    term_index = lax.axis_index("term")
    doc_index = lax.axis_index("doc")
    query_part = query_slice(query_terms, query_levels, width, term_index * width)
    local_slot = feedback_ids - doc_index * doc_rows
    positions = lax.iota(jnp.int32, doc_rows)
    selector = (local_slot[:, :, None] == positions[None, None, :]).astype(f32)
    first_all = lax.psum(dot_nt(query_part.astype(bf16), postings), "term")
    first_scores = lax.dynamic_slice_in_dim(first_all, term_index * group_rows, group_rows, 0)
    feedback = jnp.sum(selector * first_all[:, None, :], axis=2).astype(bf16).astype(f32)
    mixing = jnp.sum(selector * feedback[:, :, None], axis=1).astype(bf16)
    numerator = jnp.dot(mixing, postings, preferred_element_type=f32)
    numerator, weight_sum = lax.psum((numerator, jnp.sum(feedback, axis=1)), "doc")
    expanded = (query_part + expansion_weight * numerator / weight_sum[:, None]).astype(bf16)
    final_scores = lax.psum_scatter(
        dot_nt(expanded, postings), "term", scatter_dimension=0, tiled=True
    )
    return first_scores, final_scores


def per_device(postings, query_terms, query_levels, feedback_ids):
    docs, width = postings.shape
    queries, slots = query_terms.shape
    fits = (
        lax.axis_size("doc") == 8
        and lax.axis_size("term") > 1
        and queries == LANES
        and queries % (8 * lax.axis_size("term")) == 0
        and width % LANES == 0
        and docs % LANES == 0
    )
    run = fused if fits else general
    return run(postings, query_terms, query_levels, feedback_ids)


def solution(mesh):
    return jax.shard_map(
        per_device,
        mesh=mesh,
        in_specs=(P("doc", "term"), P(), P(), P()),
        out_specs=(P("term", "doc"), P("term", "doc")),
        check_vma=False,
    )
```

time: 369 us -> 68.6 us (0.19)
  other arithmetic: 170 us -> 0 us
  waiting for transfers between devices: 122 us -> 0 us
  Pallas kernels: 0 us -> 63.4 us
  matrix products: 23.2 us -> 0 us
  local copies, waits for them, and re-layouts: 23.6 us -> 3.7 us
  between operations: 13.8 us -> 0.64 us
  blocking collectives: 12.4 us -> 0 us
    add x64 -> x0, other arithmetic: 146 us -> none  [the longest x32 146 us: add_term(): return total + jnp.where(ids_now == columns[None, :], weight_now, 0.0)]
    psum x2 -> x0, waiting for transfers between devices: 104 us -> none  [the longest x1 65.6 us: per_device(): numerator_all, weight_sum = lax.psum((numerator, weight_part), 'doc')]
    pallas_call x0 -> x1, Pallas kernels: none -> 63.4 us  [fused(): pl.pallas_call(functools.partial(fused_kernel, n_term, n_doc, chunks), ou...]
    dot_general x3 -> x0, matrix products: 23.2 us -> none  [the longest x2 16.8 us: score_block(): lax.dot_general(query_rows, postings, (((1,), (1,)), ((), ())), preferred...]
    broadcast_in_dim x32 -> x0, other arithmetic: 22.2 us -> none  [add_term(): return total + jnp.where(ids_now == columns[None, :], weight_now, 0.0)]
    eq x32 -> x0, local copies, waits for them, and re-layouts: 22.1 us -> none  [add_term(): return total + jnp.where(ids_now == columns[None, :], weight_now, 0.0)]
    reduce_scatter x1 -> x0, waiting for transfers between devices: 18.4 us -> none  [per_device(): lax.psum_scatter(score_block(expanded, postings), 'term', scatter_dimensi...]
    psum x1 -> x0, blocking collectives: 12.4 us -> none  [per_device(): numerator_all, weight_sum = lax.psum((numerator, weight_part), 'doc')]
  transfers between devices with their start and end apart: 3 -> 0, of which waited for: 3 -> 0; matrix products, arithmetic and copies ran while one was open for 0% -> 0% of each run, Pallas kernels for 0% -> 0%
where the time goes in v1:
time: 68.6 us; the launch traced here: 67.7 us
  Pallas kernels  63.4 us (92%)
  local copies, waits for them, and re-layouts  3.7 us (5%)
    pallas_call x1, Pallas kernels, fused(): pl.pallas_call(functools.partial(fused_kernel, n_term, n_doc, chunks), ou...  63.4 us
    unnamed x5, local copies, waits for them, and re-layouts  3.7 us

profile of v1, /device:TPU:0, one launch (start us, length us, event | category | flops | bytes accessed | tf_op | source)
XLA Modules:
  0.0 67.7 jit_solution(2730434678269540595)
XLA Ops:
  0.6 0.8 %copy.6.terms = s32[128,32]{1,0:T(8,128)S(1)} copy(s32[128,32]{0,1:T(8,128)} %param.5) | data formatting | bytes 32768 | tf_op args[1]
  1.4 0.8 %copy.7.levels = s32[128,32]{1,0:T(8,128)S(1)} copy(s32[128,32]{0,1:T(8,128)} %param.6) | data formatting | bytes 32768 | tf_op args[2]
  2.3 0.8 %copy.8.ids = s32[128,10]{1,0:T(8,128)S(1)} copy(s32[128,10]{0,1:T(8,128)} %param.7) | data formatting | bytes 10240 | tf_op args[3]
  3.1 63.4 %fused_feedback.1 = (f32[32,512]{1,0:T(8,128)S(1)}, f32[32,512]{1,0:T(8,128)S(1)}) custom-call(bf16[512,7680]{1,0:T(8,128)(2,1)} %postings.1, s32[128,32]{1,0:T(8,128)S(1)} %copy.6.terms, s32[128,32]{1,0:T(8,128)S(1)} %copy.7.levels, s32[128,10]{1,0:T(8,128)S(1)} %copy.8.ids), custom_call_target="tpu_custom_call" | custom-call | flops 3019898880 | bytes 7864320 | tf_op jit(solution)/shard_map/fused_feedback/pallas_call | solution.py:323
  66.5 0.6 copy.11
  67.1 0.6 copy.12

commit v2 on v1

--- a/solution.py
+++ b/solution.py
@@ -19,20 +19,48 @@
     return lax.dot_general(a, b, NT, preferred_element_type=f32)
 
 
+def plan(chunks, mega):
+    part = mega / chunks
+    send = (part * 0.83, part * 5.0, part * 2.5, part * 2.5, part * 5.0, part * 0.83)
+    work = (3.0 / chunks, 1.0 / chunks, 0.5 / chunks, 1.0 / chunks, 0.02, 0.02, 4.0 / chunks)
+    free = {"twin": 0.0, "x": 0.0, "y": 0.0}
+    arrival, at, order = {}, [0] * 7, []
+    now = 0.0
+    rank = (5, 4, 3, 2, 1, 0, 6)
+
+    def due(k):
+        return 0.0 if k == 0 else arrival.get((k - 1, at[k]), float("inf"))
+
+    while at[6] < chunks:
+        open_steps = [k for k in rank if at[k] < chunks]
+        ready = [k for k in open_steps if due(k) <= now]
+        k = ready[0] if ready else min(open_steps, key=due)
+        c = at[k]
+        now = max(now, due(k)) + work[k]
+        if k < 6:
+            link = "twin" if k in (0, 5) else "xy"[(c + (k in (2, 3))) % 2]
+            free[link] = max(now, free[link]) + send[k]
+            arrival[k, c] = free[link] + 1.0
+        at[k] += 1
+        order.append((k, c))
+    return order
+
+
 def fused_kernel(
-    n_term, n_doc, chunks,
+    n_term, n_doc, chunks, loads,
     postings, terms, levels, ids, first_out, final_out,
     p_ref, q_ref, hi_ref, lo_ref, lev_ref, part_ref, sel_ref, mix_ref,
     fb_ref, first_ref, ws_ref, wcol_ref, nb_ref, tw_ref, s1_ref, a_ref, s2_ref, b_ref,
-    e_ref, acc_ref, last_ref,
+    e_ref, acc_ref, code_ref, last_ref, top_ref, tops_ref,
     p_sem, fb_send, fb_recv, first_send, first_recv, ws_send, ws_recv,
-    pipe_send, pipe_recv, last_send, last_recv,
+    pipe_send, pipe_recv, last_send, last_recv, top_send, top_recv,
 ):
     t = lax.axis_index("term")
     d = lax.axis_index("doc")
     docs, width = p_ref.shape
-    queries, slots = terms.shape
+    slots, queries = terms.shape
     cw = width // chunks
+    lw = width // loads
     his = width // LANES
     rows_out = queries // n_term
     half, quarter, eighth = queries // 2, queries // 4, queries // 8
@@ -44,10 +72,14 @@
     def cols(c):
         return pl.ds(pl.multiple_of(c * cw, LANES), cw)
 
+    def load_cols(c):
+        return pl.ds(pl.multiple_of(c * lw, LANES), lw)
+
     def load(c):
-        return pltpu.make_async_copy(postings.at[:, cols(c)], p_ref.at[:, cols(c)], p_sem.at[c])
-
-    for c in range(chunks):
+        here = load_cols(c)
+        return pltpu.make_async_copy(postings.at[:, here], p_ref.at[:, here], p_sem.at[c])
+
+    for c in range(loads):
         load(c).start()
 
     barrier = pltpu.get_barrier_semaphore()
@@ -67,7 +99,9 @@
     )
 
     def lay(values):
-        wide = jnp.dot(values.astype(f32).astype(bf16), spread, preferred_element_type=f32)
+        wide = lax.dot_general(
+            values.astype(f32).astype(bf16), spread, (((0,), (0,)), ((), ())), preferred_element_type=f32
+        )
         return jnp.sum(jnp.where(own, wide, 0.0).reshape(queries // 8, 8, group), axis=1)
 
     ids_now = terms[...]
@@ -80,7 +114,7 @@
     row_code = lax.broadcasted_iota(jnp.int32, (his * 8, group), 0).astype(f32)
     lane_code = lax.broadcasted_iota(jnp.int32, (LANES, group), 0).astype(f32)
 
-    def build(g, carry):
+    def build_one(g):
         left = jnp.where(
             hi_ref[pl.ds(g, 1), :] == row_code, lev_ref[pl.ds(g, 1), :], 0.0
         ).astype(bf16)
@@ -89,12 +123,16 @@
         rows = pl.ds(pl.multiple_of(g * 8, 8), 8)
         for h in range(his):
             q_ref[rows, h * LANES : (h + 1) * LANES] = block[h * 8 : (h + 1) * 8]
+
+    def build(g, carry):
+        for i in range(4):
+            build_one(g * 4 + i)
         return carry
 
-    lax.fori_loop(0, queries // 8, build, 0)
+    lax.fori_loop(0, queries // 32, build, 0)
 
     place = lax.broadcasted_iota(jnp.int32, (queries, docs), 1)
-    local = ids[...] - d * docs
+    local = ids[...].T - d * docs
     sel = place == local[:, 0:1]
     for j in range(1, local.shape[1]):
         sel = sel | (place == local[:, j : j + 1])
@@ -104,10 +142,10 @@
 
     def score(c, carry):
         load(c).wait()
-        part_ref[...] += dot_nt(q_ref[:, cols(c)].astype(bf16), p_ref[:, cols(c)])
+        part_ref[...] += dot_nt(q_ref[:, load_cols(c)].astype(bf16), p_ref[:, load_cols(c)])
         return carry
 
-    lax.fori_loop(0, chunks, score, 0)
+    lax.fori_loop(0, loads, score, 0)
 
     pl.semaphore_wait(barrier, n_term + n_doc - 2)
 
@@ -130,9 +168,15 @@
     def last_copy(o):
         peer = (t + o) % n_term
         return pltpu.make_async_remote_copy(
-            acc_ref.at[pl.ds(pl.multiple_of(peer * rows_out, 8), rows_out), :], last_ref.at[t],
+            code_ref.at[pl.ds(pl.multiple_of(peer * rows_out, 16), rows_out), :], last_ref.at[t],
             last_send.at[o - 1], last_recv.at[o - 1],
             device_id={"term": peer}, device_id_type=MESH,
+        )
+
+    def top_copy(o):
+        return pltpu.make_async_remote_copy(
+            top_ref.at[t], top_ref.at[t], top_send.at[o - 1], top_recv.at[o - 1],
+            device_id={"term": (t + o) % n_term}, device_id_type=MESH,
         )
 
     def ws_copy(o):
@@ -200,13 +244,10 @@
         return copy_of(5, c, at, at, twin)
 
     acc_ref[...] = jnp.zeros_like(acc_ref)
-
-    def stage(step, s, body):
-        c = s - step
-
-        @pl.when((c >= 0) & (c < chunks))
-        def _():
-            body(c)
+    eye = (
+        lax.broadcasted_iota(jnp.int32, (queries, queries), 0)
+        == lax.broadcasted_iota(jnp.int32, (queries, queries), 1)
+    )
 
     def step1(c):
         exchange(0, c).wait_recv()
@@ -253,32 +294,30 @@
         here = cols(c)
         acc_ref[...] += dot_nt(e_ref[:, here], p_ref[:, here])
 
-    def pipeline(s, carry):
-        @pl.when(s == 3)
-        def _():
-            for o in range(1, n_doc):
-                ws_copy(o).wait_recv()
-            total = ws_ref[0]
-            for o in range(1, n_doc):
-                total = total + ws_ref[o]
-            shape = (queries, queries)
-            eye = lax.broadcasted_iota(jnp.int32, shape, 0) == lax.broadcasted_iota(jnp.int32, shape, 1)
-            column = jnp.sum(jnp.where(eye, total[0:1, :], 0.0), axis=1, keepdims=True)
-            wcol_ref[...] = jnp.broadcast_to(column, wcol_ref.shape)
-
-        stage(5, s, step5)
-        stage(4, s, step4)
-        stage(3, s, step3)
-        stage(2, s, step2)
-        stage(1, s, step1)
-        stage(0, s, step0)
-        stage(6, s, step6)
-        return carry
-
-    lax.fori_loop(0, chunks + 6, pipeline, 0)
-
+    def weights():
+        for o in range(1, n_doc):
+            ws_copy(o).wait_recv()
+        total = ws_ref[0]
+        for o in range(1, n_doc):
+            total = total + ws_ref[o]
+        column = jnp.sum(jnp.where(eye, total[0:1, :], 0.0), axis=1, keepdims=True)
+        wcol_ref[...] = jnp.broadcast_to(column, wcol_ref.shape)
+
+    body = (step0, step1, step2, step3, step4, step5, step6)
+    for k, c in plan(chunks, queries * width * 2e-6):
+        if (k, c) == (3, 0):
+            weights()
+        body[k](c)
+
+    top = jnp.maximum(jnp.max(acc_ref[...], axis=1, keepdims=True), 1e-30)
+    code_ref[...] = jnp.round(acc_ref[...] * (32767.0 / top)).astype(jnp.int32).astype(jnp.int16)
     for o in range(1, n_term):
         last_copy(o).start()
+    top_ref[t] = jnp.broadcast_to(
+        jnp.sum(jnp.where(eye, top, 0.0), axis=0, keepdims=True) / 32767.0, (8, queries)
+    )
+    for o in range(1, n_term):
+        top_copy(o).start()
 
     for o in range(1, n_term):
         first_copy(o).wait_recv()
@@ -287,18 +326,25 @@
         total = total + first_ref[s]
     first_out[...] = total
 
-    last_ref[t] = acc_ref[own_rows, :]
+    for o in range(1, n_term):
+        top_copy(o).wait_recv()
+    for s in range(n_term):
+        column = jnp.sum(jnp.where(eye, top_ref[s][0:1, :], 0.0), axis=1, keepdims=True)
+        wcol_ref[...] = jnp.broadcast_to(column, wcol_ref.shape)
+        tops_ref[s] = wcol_ref[own_rows, :]
+    total = acc_ref[own_rows, :]
     for o in range(1, n_term):
         last_copy(o).wait_recv()
-    total = last_ref[0]
-    for s in range(1, n_term):
-        total = total + last_ref[s]
+        s = (t + n_term - o) % n_term
+        steps = last_ref[s].astype(jnp.int32).astype(f32)
+        total = total + steps * tops_ref[s][:, 0:1]
     final_out[...] = total
 
     for o in range(1, n_term):
         fb_copy(o).wait_send()
         first_copy(o).wait_send()
         last_copy(o).wait_send()
+        top_copy(o).wait_send()
     for o in range(1, n_doc):
         ws_copy(o).wait_send()
 
@@ -314,14 +360,15 @@
     docs, width = postings.shape
     queries, slots = query_terms.shape
     n_term, n_doc = lax.axis_size("term"), lax.axis_size("doc")
-    chunks = next(c for c in (6, 4, 2, 1) if width % (c * LANES) == 0)
+    chunks = next(c for c in (10, 6, 4, 2, 1) if width % (c * LANES) == 0)
+    loads = next(c for c in (5, 3, 2, 1) if width % (c * LANES) == 0)
     rows_out = queries // n_term
     group = 8 * slots
     vmem = pltpu.VMEM
     dma = pltpu.SemaphoreType.DMA
     out = jax.ShapeDtypeStruct((rows_out, docs), f32)
     return pl.pallas_call(
-        functools.partial(fused_kernel, n_term, n_doc, chunks),
+        functools.partial(fused_kernel, n_term, n_doc, chunks, loads),
         out_shape=(out, out),
         in_specs=[pl.BlockSpec(memory_space=pl.ANY)] + [pl.BlockSpec(memory_space=pltpu.VMEM)] * 3,
         out_specs=(pl.BlockSpec(memory_space=pltpu.VMEM),) * 2,
@@ -346,8 +393,11 @@
             vmem((queries // 8, width), bf16),
             vmem((queries, width), bf16),
             vmem((queries, docs), f32),
-            vmem((n_term, rows_out, docs), f32),
-            dma((chunks,)),
+            vmem((queries, docs), jnp.int16),
+            vmem((n_term, rows_out, docs), jnp.int16),
+            vmem((n_term, 8, queries), f32),
+            vmem((n_term, rows_out, LANES), f32),
+            dma((loads,)),
             dma((n_term - 1,)),
             dma((n_term - 1,)),
             dma((n_term - 1,)),
@@ -356,6 +406,8 @@
             dma((n_doc - 1,)),
             dma((6, chunks)),
             dma((6, chunks)),
+            dma((n_term - 1,)),
+            dma((n_term - 1,)),
             dma((n_term - 1,)),
             dma((n_term - 1,)),
         ],
@@ -366,7 +418,7 @@
             flops=6 * queries * docs * width, bytes_accessed=2 * docs * width, transcendentals=0
         ),
         name="fused_feedback",
-    )(postings, query_terms, query_levels, feedback_ids)
+    )(postings, query_terms.T, query_levels.T, feedback_ids.T)
 
 
 def query_slice(query_terms, query_levels, width, offset):
@@ -413,7 +465,7 @@
         lax.axis_size("doc") == 8
         and lax.axis_size("term") > 1
         and queries == LANES
-        and queries % (8 * lax.axis_size("term")) == 0
+        and queries % (16 * lax.axis_size("term")) == 0
         and width % LANES == 0
         and docs % LANES == 0
     )

time: 68.6 us -> 48.5 us (0.71)
  Pallas kernels: 63.4 us -> 44.1 us
    pallas_call x1, Pallas kernels: 63.4 us -> 44.1 us  [fused(): pl.pallas_call(functools.partial(fused_kernel, n_term, n_doc, chunks, loa...]
    unnamed x5 -> x8, local copies, waits for them, and re-layouts: 3.7 us -> 3.38 us
where the time goes in v2:
time: 48.5 us; the launch traced here: 48.1 us
  Pallas kernels  44.1 us (91%)
  local copies, waits for them, and re-layouts  3.38 us (7%)
  between operations  0.65 us (1%)
    pallas_call x1, Pallas kernels, fused(): pl.pallas_call(functools.partial(fused_kernel, n_term, n_doc, chunks, loa...  44.1 us
    unnamed x8, local copies, waits for them, and re-layouts  3.38 us

profile of v2, /device:TPU:0, one launch (start us, length us, event | category | flops | bytes accessed | tf_op | source)
XLA Modules:
  0.0 48.1 jit_solution(10515313501329722336)
XLA Ops:
  0.6 0.0 copy-start
  0.6 0.7 %copy-done = s32[128,32]{0,1:T(8,128)S(1)} copy-done((s32[128,32]{0,1:T(8,128)S(1)}, s32[128,32]{0,1:T(8,128)}, u32[]{:S(2)}) %copy-start) | copy-done | bytes 16408
  1.3 0.0 copy-start.1
  1.4 0.7 %copy-done.1 = s32[128,32]{0,1:T(8,128)S(1)} copy-done((s32[128,32]{0,1:T(8,128)S(1)}, s32[128,32]{0,1:T(8,128)}, u32[]{:S(2)}) %copy-start.1) | copy-done | bytes 16408
  2.1 0.0 copy-start.2
  2.1 0.7 %copy-done.2 = s32[128,10]{0,1:T(8,128)S(1)} copy-done((s32[128,10]{0,1:T(8,128)S(1)}, s32[128,10]{0,1:T(8,128)}, u32[]{:S(2)}) %copy-start.2) | copy-done | bytes 5144
  2.8 44.1 %fused_feedback.1 = (f32[32,512]{1,0:T(8,128)S(1)}, f32[32,512]{1,0:T(8,128)S(1)}) custom-call(bf16[512,7680]{1,0:T(8,128)(2,1)} %postings.1, s32[32,128]{1,0:T(8,128)S(1)} %bitcast.3, s32[32,128]{1,0:T(8,128)S(1)} %bitcast.4, s32[10,128]{1,0:T(8,128)S(1)} %bitcast.5), custom_call_target="tpu_custom_call" | custom-call | flops 3019898880 | bytes 7864320 | tf_op jit(solution)/shard_map/fused_feedback/pallas_call | solution.py:370
  46.8 0.6 %copy.8 = f32[32,512]{1,0:T(8,128)} copy(f32[32,512]{1,0:T(8,128)S(1)} %get-tuple-element.4) | data formatting | bytes 131072
  47.5 0.6 %copy.9 = f32[32,512]{1,0:T(8,128)} copy(f32[32,512]{1,0:T(8,128)S(1)} %get-tuple-element.5) | data formatting | bytes 131072
Async XLA Ops:
  0.6 0.7 %copy-start = (s32[128,32]{0,1:T(8,128)S(1)}, s32[128,32]{0,1:T(8,128)}, u32[]{:S(2)}) copy-start(s32[128,32]{0,1:T(8,128)} %param.5) | copy-start | bytes 49156
  1.3 0.7 %copy-start.1 = (s32[128,32]{0,1:T(8,128)S(1)}, s32[128,32]{0,1:T(8,128)}, u32[]{:S(2)}) copy-start(s32[128,32]{0,1:T(8,128)} %param.6) | copy-start | bytes 49156
  2.1 0.7 %copy-start.2 = (s32[128,10]{0,1:T(8,128)S(1)}, s32[128,10]{0,1:T(8,128)}, u32[]{:S(2)}) copy-start(s32[128,10]{0,1:T(8,128)} %param.7) | copy-start | bytes 15364

commit v3 on v2

--- a/solution.py
+++ b/solution.py
@@ -49,7 +49,7 @@
 def fused_kernel(
     n_term, n_doc, chunks, loads,
     postings, terms, levels, ids, first_out, final_out,
-    p_ref, q_ref, hi_ref, lo_ref, lev_ref, part_ref, sel_ref, mix_ref,
+    p_ref, q_ref, hi_ref, lo_ref, lev_ref, part_ref, tall_ref, sel_ref, mix_ref,
     fb_ref, first_ref, ws_ref, wcol_ref, nb_ref, tw_ref, s1_ref, a_ref, s2_ref, b_ref,
     e_ref, acc_ref, code_ref, last_ref, top_ref, tops_ref,
     p_sem, fb_send, fb_recv, first_send, first_recv, ws_send, ws_recv,
@@ -138,14 +138,15 @@
         sel = sel | (place == local[:, j : j + 1])
     sel_ref[...] = jnp.where(sel, 1.0, 0.0)
 
-    part_ref[...] = jnp.zeros_like(part_ref)
+    tall_ref[...] = jnp.zeros_like(tall_ref)
 
     def score(c, carry):
         load(c).wait()
-        part_ref[...] += dot_nt(q_ref[:, load_cols(c)].astype(bf16), p_ref[:, load_cols(c)])
+        tall_ref[...] += dot_nt(p_ref[:, load_cols(c)], q_ref[:, load_cols(c)].astype(bf16))
         return carry
 
     lax.fori_loop(0, loads, score, 0)
+    part_ref[...] = tall_ref[...].T
 
     pl.semaphore_wait(barrier, n_term + n_doc - 2)
 
@@ -243,7 +244,7 @@
         at = e_ref.at[rows(base, half), here]
         return copy_of(5, c, at, at, twin)
 
-    acc_ref[...] = jnp.zeros_like(acc_ref)
+    tall_ref[...] = jnp.zeros_like(tall_ref)
     eye = (
         lax.broadcasted_iota(jnp.int32, (queries, queries), 0)
         == lax.broadcasted_iota(jnp.int32, (queries, queries), 1)
@@ -292,7 +293,7 @@
     def step6(c):
         exchange(5, c).wait_recv()
         here = cols(c)
-        acc_ref[...] += dot_nt(e_ref[:, here], p_ref[:, here])
+        tall_ref[...] += dot_nt(p_ref[:, here], e_ref[:, here])
 
     def weights():
         for o in range(1, n_doc):
@@ -309,6 +310,7 @@
             weights()
         body[k](c)
 
+    acc_ref[...] = tall_ref[...].T
     top = jnp.maximum(jnp.max(acc_ref[...], axis=1, keepdims=True), 1e-30)
     code_ref[...] = jnp.round(acc_ref[...] * (32767.0 / top)).astype(jnp.int32).astype(jnp.int16)
     for o in range(1, n_term):
@@ -379,6 +381,7 @@
             vmem((queries // 8, group), f32),
             vmem((queries // 8, group), f32),
             vmem((queries, docs), f32),
+            vmem((docs, queries), f32),
             vmem((queries, docs), f32),
             vmem((queries, docs), bf16),
             vmem((n_term, 8, docs), f32),

time: 48.5 us -> 48.8 us (level)
  no operation moved by 1% of the time
where the time goes in v3:
time: 48.8 us; the launch traced here: 48.3 us
  Pallas kernels  44.3 us (91%)
  local copies, waits for them, and re-layouts  3.38 us (7%)
  between operations  0.65 us (1%)
    pallas_call x1, Pallas kernels, fused(): pl.pallas_call(functools.partial(fused_kernel, n_term, n_doc, chunks, loa...  44.3 us
    unnamed x8, local copies, waits for them, and re-layouts  3.38 us

profile of v3, /device:TPU:0, one launch (start us, length us, event | category | flops | bytes accessed | tf_op | source)
XLA Modules:
  0.0 48.3 jit_solution(7319925834707352238)
XLA Ops:
  0.6 0.0 copy-start
  0.6 0.7 %copy-done = s32[128,32]{0,1:T(8,128)S(1)} copy-done((s32[128,32]{0,1:T(8,128)S(1)}, s32[128,32]{0,1:T(8,128)}, u32[]{:S(2)}) %copy-start) | copy-done | bytes 16408
  1.3 0.0 copy-start.1
  1.4 0.7 %copy-done.1 = s32[128,32]{0,1:T(8,128)S(1)} copy-done((s32[128,32]{0,1:T(8,128)S(1)}, s32[128,32]{0,1:T(8,128)}, u32[]{:S(2)}) %copy-start.1) | copy-done | bytes 16408
  2.1 0.0 copy-start.2
  2.1 0.7 %copy-done.2 = s32[128,10]{0,1:T(8,128)S(1)} copy-done((s32[128,10]{0,1:T(8,128)S(1)}, s32[128,10]{0,1:T(8,128)}, u32[]{:S(2)}) %copy-start.2) | copy-done | bytes 5144
  2.8 44.3 %fused_feedback.1 = (f32[32,512]{1,0:T(8,128)S(1)}, f32[32,512]{1,0:T(8,128)S(1)}) custom-call(bf16[512,7680]{1,0:T(8,128)(2,1)} %postings.1, s32[32,128]{1,0:T(8,128)S(1)} %bitcast.3, s32[32,128]{1,0:T(8,128)S(1)} %bitcast.4, s32[10,128]{1,0:T(8,128)S(1)} %bitcast.5), custom_call_target="tpu_custom_call" | custom-call | flops 3019898880 | bytes 7864320 | tf_op jit(solution)/shard_map/fused_feedback/pallas_call | solution.py:372
  47.1 0.6 %copy.8 = f32[32,512]{1,0:T(8,128)} copy(f32[32,512]{1,0:T(8,128)S(1)} %get-tuple-element.4) | data formatting | bytes 131072
  47.7 0.6 %copy.9 = f32[32,512]{1,0:T(8,128)} copy(f32[32,512]{1,0:T(8,128)S(1)} %get-tuple-element.5) | data formatting | bytes 131072
Async XLA Ops:
  0.6 0.7 %copy-start = (s32[128,32]{0,1:T(8,128)S(1)}, s32[128,32]{0,1:T(8,128)}, u32[]{:S(2)}) copy-start(s32[128,32]{0,1:T(8,128)} %param.5) | copy-start | bytes 49156
  1.3 0.7 %copy-start.1 = (s32[128,32]{0,1:T(8,128)S(1)}, s32[128,32]{0,1:T(8,128)}, u32[]{:S(2)}) copy-start(s32[128,32]{0,1:T(8,128)} %param.6) | copy-start | bytes 49156
  2.1 0.7 %copy-start.2 = (s32[128,10]{0,1:T(8,128)S(1)}, s32[128,10]{0,1:T(8,128)}, u32[]{:S(2)}) copy-start(s32[128,10]{0,1:T(8,128)} %param.7) | copy-start | bytes 15364

commit v4 on v2

--- a/solution.py
+++ b/solution.py
@@ -10,6 +10,7 @@
 expansion_weight = 0.25
 MESH = pl.DeviceIdType.MESH
 LANES = 128
+BIN = 256
 NT = (((1,), (1,)), ((), ()))
 f32 = jnp.float32
 bf16 = jnp.bfloat16
@@ -48,7 +49,7 @@
 
 def fused_kernel(
     n_term, n_doc, chunks, loads,
-    postings, terms, levels, ids, first_out, final_out,
+    slots, postings, small, first_out, final_out,
     p_ref, q_ref, hi_ref, lo_ref, lev_ref, part_ref, sel_ref, mix_ref,
     fb_ref, first_ref, ws_ref, wcol_ref, nb_ref, tw_ref, s1_ref, a_ref, s2_ref, b_ref,
     e_ref, acc_ref, code_ref, last_ref, top_ref, tops_ref,
@@ -58,10 +59,10 @@
     t = lax.axis_index("term")
     d = lax.axis_index("doc")
     docs, width = p_ref.shape
-    slots, queries = terms.shape
+    queries = small.shape[1]
     cw = width // chunks
     lw = width // loads
-    his = width // LANES
+    his = width // BIN
     rows_out = queries // n_term
     half, quarter, eighth = queries // 2, queries // 4, queries // 8
 
@@ -104,15 +105,15 @@
         )
         return jnp.sum(jnp.where(own, wide, 0.0).reshape(queries // 8, 8, group), axis=1)
 
-    ids_now = terms[...]
+    ids_now = small[:slots]
     q8 = (lax.broadcasted_iota(jnp.int32, (queries // 8, group), 1) // slots).astype(f32)
-    hi = lay(ids_now // LANES) - (t * his).astype(f32)
+    hi = lay(ids_now // BIN) - (t * his).astype(f32)
     hi_ref[...] = hi * 8.0 + q8
-    lo_ref[...] = lay(ids_now % LANES)
-    lev_ref[...] = lay(levels[...])
+    lo_ref[...] = lay(ids_now % BIN)
+    lev_ref[...] = lay(small[slots : 2 * slots])
 
     row_code = lax.broadcasted_iota(jnp.int32, (his * 8, group), 0).astype(f32)
-    lane_code = lax.broadcasted_iota(jnp.int32, (LANES, group), 0).astype(f32)
+    lane_code = lax.broadcasted_iota(jnp.int32, (BIN, group), 0).astype(f32)
 
     def build_one(g):
         left = jnp.where(
@@ -122,7 +123,7 @@
         block = dot_nt(left, right) * 0.01
         rows = pl.ds(pl.multiple_of(g * 8, 8), 8)
         for h in range(his):
-            q_ref[rows, h * LANES : (h + 1) * LANES] = block[h * 8 : (h + 1) * 8]
+            q_ref[rows, h * BIN : (h + 1) * BIN] = block[h * 8 : (h + 1) * 8]
 
     def build(g, carry):
         for i in range(4):
@@ -132,7 +133,7 @@
     lax.fori_loop(0, queries // 32, build, 0)
 
     place = lax.broadcasted_iota(jnp.int32, (queries, docs), 1)
-    local = ids[...].T - d * docs
+    local = small[2 * slots :].T - d * docs
     sel = place == local[:, 0:1]
     for j in range(1, local.shape[1]):
         sel = sel | (place == local[:, j : j + 1])
@@ -327,6 +328,19 @@
     first_out[...] = total
 
     for o in range(1, n_term):
+        fb_copy(o).wait_send()
+        first_copy(o).wait_send()
+    for o in range(1, n_doc):
+        ws_copy(o).wait_send()
+
+    def drain(c, carry):
+        for step in range(6):
+            exchange(step, c).wait_send()
+        return carry
+
+    lax.fori_loop(0, chunks, drain, 0)
+
+    for o in range(1, n_term):
         top_copy(o).wait_recv()
     for s in range(n_term):
         column = jnp.sum(jnp.where(eye, top_ref[s][0:1, :], 0.0), axis=1, keepdims=True)
@@ -341,19 +355,8 @@
     final_out[...] = total
 
     for o in range(1, n_term):
-        fb_copy(o).wait_send()
-        first_copy(o).wait_send()
         last_copy(o).wait_send()
         top_copy(o).wait_send()
-    for o in range(1, n_doc):
-        ws_copy(o).wait_send()
-
-    def drain(c, carry):
-        for step in range(6):
-            exchange(step, c).wait_send()
-        return carry
-
-    lax.fori_loop(0, chunks, drain, 0)
 
 
 def fused(postings, query_terms, query_levels, feedback_ids):
@@ -368,9 +371,9 @@
     dma = pltpu.SemaphoreType.DMA
     out = jax.ShapeDtypeStruct((rows_out, docs), f32)
     return pl.pallas_call(
-        functools.partial(fused_kernel, n_term, n_doc, chunks, loads),
+        functools.partial(fused_kernel, n_term, n_doc, chunks, loads, slots),
         out_shape=(out, out),
-        in_specs=[pl.BlockSpec(memory_space=pl.ANY)] + [pl.BlockSpec(memory_space=pltpu.VMEM)] * 3,
+        in_specs=[pl.BlockSpec(memory_space=pl.ANY), pl.BlockSpec(memory_space=pltpu.VMEM)],
         out_specs=(pl.BlockSpec(memory_space=pltpu.VMEM),) * 2,
         scratch_shapes=[
             vmem((docs, width), bf16),
@@ -418,7 +421,7 @@
             flops=6 * queries * docs * width, bytes_accessed=2 * docs * width, transcendentals=0
         ),
         name="fused_feedback",
-    )(postings, query_terms.T, query_levels.T, feedback_ids.T)
+    )(postings, jnp.concatenate([query_terms.T, query_levels.T, feedback_ids.T]))
 
 
 def query_slice(query_terms, query_levels, width, offset):
@@ -466,7 +469,7 @@
         and lax.axis_size("term") > 1
         and queries == LANES
         and queries % (16 * lax.axis_size("term")) == 0
-        and width % LANES == 0
+        and width % BIN == 0
         and docs % LANES == 0
     )
     run = fused if fits else general

time: 48.5 us -> 46.6 us (0.961)
  local copies, waits for them, and re-layouts: 3.38 us -> 1.26 us
  other arithmetic: 0 us -> 0.76 us
  Pallas kernels: 44.1 us -> 43.6 us
    unnamed x8 -> x2, local copies, waits for them, and re-layouts: 3.38 us -> 1.26 us
    concatenate x0 -> x1, other arithmetic: none -> 0.76 us  [fused(): jnp.concatenate([query_terms.T, query_levels.T, feedback_ids.T])]
where the time goes in v4:
time: 46.6 us; the launch traced here: 46.3 us
  Pallas kernels  43.6 us (94%)
  local copies, waits for them, and re-layouts  1.26 us (3%)
  other arithmetic  0.76 us (2%)
  between operations  0.64 us (1%)
    pallas_call x1, Pallas kernels, fused(): pl.pallas_call(functools.partial(fused_kernel, n_term, n_doc, chunks, loa...  43.6 us
    unnamed x2, local copies, waits for them, and re-layouts  1.26 us

profile of v4, /device:TPU:0, one launch (start us, length us, event | category | flops | bytes accessed | tf_op | source)
XLA Modules:
  0.0 46.3 jit_solution(714093145886042158)
XLA Ops:
  0.6 0.8 %pad_add_fusion.small = s32[74,128]{1,0:T(8,128)S(1)} fusion(s32[10,128]{1,0:T(8,128)} %bitcast.5, s32[32,128]{1,0:T(8,128)} %bitcast.3, s32[32,128]{1,0:T(8,128)} %bitcast.4), kind=kLoop, calls=%fused_computation | loop fusion | flops 18944 | bytes 75776 | tf_op jit(solution)/shard_map/concatenate | solution.py:424
  1.4 43.6 %fused_feedback.1 = (f32[32,512]{1,0:T(8,128)S(1)}, f32[32,512]{1,0:T(8,128)S(1)}) custom-call(bf16[512,7680]{1,0:T(8,128)(2,1)} %postings.1, s32[74,128]{1,0:T(8,128)S(1)} %pad_add_fusion.small), custom_call_target="tpu_custom_call" | custom-call | flops 3019898880 | bytes 7864320 | tf_op jit(solution)/shard_map/fused_feedback/pallas_call | solution.py:373
  45.0 0.6 %copy.8 = f32[32,512]{1,0:T(8,128)} copy(f32[32,512]{1,0:T(8,128)S(1)} %get-tuple-element.4) | data formatting | bytes 131072
  45.6 0.6 %copy.9 = f32[32,512]{1,0:T(8,128)} copy(f32[32,512]{1,0:T(8,128)S(1)} %get-tuple-element.5) | data formatting | bytes 131072

commit v5 on v4

--- a/solution.py
+++ b/solution.py
@@ -363,7 +363,7 @@
     docs, width = postings.shape
     queries, slots = query_terms.shape
     n_term, n_doc = lax.axis_size("term"), lax.axis_size("doc")
-    chunks = next(c for c in (10, 6, 4, 2, 1) if width % (c * LANES) == 0)
+    chunks = next(c for c in (6, 4, 2, 1) if width % (c * LANES) == 0)
     loads = next(c for c in (5, 3, 2, 1) if width % (c * LANES) == 0)
     rows_out = queries // n_term
     group = 8 * slots

time: 46.6 us -> 47 us (level)
  no operation moved by 1% of the time
where the time goes in v5:
time: 47 us; the launch traced here: 46.7 us
  Pallas kernels  44 us (94%)
  local copies, waits for them, and re-layouts  1.26 us (3%)
  other arithmetic  0.76 us (2%)
  between operations  0.64 us (1%)
    pallas_call x1, Pallas kernels, fused(): pl.pallas_call(functools.partial(fused_kernel, n_term, n_doc, chunks, loa...  44 us
    unnamed x2, local copies, waits for them, and re-layouts  1.26 us

profile of v5, /device:TPU:0, one launch (start us, length us, event | category | flops | bytes accessed | tf_op | source)
XLA Modules:
  0.0 46.7 jit_solution(10492744350178810526)
XLA Ops:
  0.6 0.8 %pad_add_fusion.small = s32[74,128]{1,0:T(8,128)S(1)} fusion(s32[10,128]{1,0:T(8,128)} %bitcast.5, s32[32,128]{1,0:T(8,128)} %bitcast.3, s32[32,128]{1,0:T(8,128)} %bitcast.4), kind=kLoop, calls=%fused_computation | loop fusion | flops 18944 | bytes 75776 | tf_op jit(solution)/shard_map/concatenate | solution.py:424
  1.4 44.0 %fused_feedback.1 = (f32[32,512]{1,0:T(8,128)S(1)}, f32[32,512]{1,0:T(8,128)S(1)}) custom-call(bf16[512,7680]{1,0:T(8,128)(2,1)} %postings.1, s32[74,128]{1,0:T(8,128)S(1)} %pad_add_fusion.small), custom_call_target="tpu_custom_call" | custom-call | flops 3019898880 | bytes 7864320 | tf_op jit(solution)/shard_map/fused_feedback/pallas_call | solution.py:373
  45.4 0.6 %copy.8 = f32[32,512]{1,0:T(8,128)} copy(f32[32,512]{1,0:T(8,128)S(1)} %get-tuple-element.4) | data formatting | bytes 131072
  46.1 0.6 %copy.9 = f32[32,512]{1,0:T(8,128)} copy(f32[32,512]{1,0:T(8,128)S(1)} %get-tuple-element.5) | data formatting | bytes 131072
